TPU v7x, 1024 devices: a whole 4x4x32 slice. The times are simulated.
1024 devices in a mesh: group: 32 (over z), local: 8 (over x, core), dp: 4 (over y).
Axes of the slice: x: 4, y: 4, z: 32, core: 2. Of those that a mesh axis runs over, the one named last changes fastest.
Arguments:
- tokens: bfloat16 [16384, 7168], P(('dp', 'group'), 'local'), parts along dimension 0, may hold values from -6 to 6
- group_ids: int32 [16384, 4], P(('dp', 'group')), parts along dimension 0, may hold values from 0 to 31, as said below
- send_slots: int32 [16384, 4], P(('dp', 'group')), parts along dimension 0, may hold values from 0 to 17, as said below
- routing_weights: float32 [16384, 4], P(('dp', 'group')), parts along dimension 0, may hold values from 0.1 to 1
- gate_proj: bfloat16 [32, 7168, 1024], P('group', 'local'), may hold values from -0.0625 to 0.0625
- up_proj: bfloat16 [32, 7168, 1024], P('group', 'local'), may hold values from -0.0625 to 0.0625
- down_proj: bfloat16 [32, 1024, 7168], P('group', None, 'local'), may hold values from -0.1875 to 0.1875
Outputs:
- mixed: bfloat16 [16384, 7168], P(('dp', 'group'), 'local'), parts along dimension 0
There are 4 independent parts, one for each index of `dp`. A program takes and returns all parts, laid end to end along the dimension named above; an argument that names none is the same for every part. Nothing has to cross between parts.
Inputs may be any that keep to these rules, and one draw needn't show every extreme that they name: `group_ids`: each row names 4 different groups. In every aligned block of 128 rows no group is named by more than 18 rows; one group, the same for all blocks of a part, is named by exactly 18 rows in every block, and the numbers of rows that name each other group differ by at most one within a block. `send_slots`: within an aligned block of 128 rows, the copies that go to the same group have different slots.
All inputs are finite; a program needn't handle non-finite values.
Results may differ from a plain program's by a relative error of at most 0.029.
Values may be sent and summed in bfloat16 or wider, within the bound.
No kernel may reach another device: no remote copies, remote signals or barrier semaphores. Data moves between devices by JAX's collectives and lax.ppermute only.
A program may use at most 32 MiB of HBM per device.

v0:
```python
import jax
import jax.numpy as jnp
from jax import lax
from jax.sharding import PartitionSpec as P


def on_device(tokens, group_ids, send_slots, routing_weights, gate_proj, up_proj, down_proj):
    groups_count = lax.axis_size("group")
    tok_rows = tokens.shape[0]
    feature_rows = tokens.shape[1]
    top_groups = group_ids.shape[1]
    send_rows = (tok_rows * top_groups + groups_count - 1) // groups_count + tok_rows // 64
    cap_rows = send_rows * groups_count
    slot_index = group_ids * send_rows + send_slots
    buffer_iota = jnp.arange(cap_rows, dtype=jnp.int32)
    matches = buffer_iota[:, None, None] == slot_index[None, :, :]
    selector = jnp.any(matches, axis=2).astype(jnp.bfloat16)
    outgoing = jnp.dot(selector, tokens, preferred_element_type=jnp.float32).astype(jnp.bfloat16)
    outgoing = outgoing.reshape(groups_count, send_rows, feature_rows)
    arrived = lax.all_to_all(outgoing, "group", split_axis=0, concat_axis=0, tiled=True).reshape(
        cap_rows, feature_rows
    )
    gate_part = jnp.dot(arrived, gate_proj[0], preferred_element_type=jnp.float32)
    up_part = jnp.dot(arrived, up_proj[0], preferred_element_type=jnp.float32)
    down_rows = down_proj[0]
    gate_share, up_share = (
        lax.psum_scatter(
            gate_part.astype(jnp.bfloat16), "local", scatter_dimension=1, tiled=True
        ).astype(jnp.float32),
        lax.psum_scatter(
            up_part.astype(jnp.bfloat16), "local", scatter_dimension=1, tiled=True
        ).astype(jnp.float32),
    )
    hidden_share = (jax.nn.silu(gate_share) * up_share).astype(jnp.bfloat16)
    expert_out = jnp.dot(
        lax.all_gather(hidden_share, "local", axis=1, tiled=True),
        down_rows,
        preferred_element_type=jnp.float32,
    )
    expert_out = expert_out.astype(jnp.bfloat16).reshape(groups_count, send_rows, feature_rows)
    returned = lax.all_to_all(expert_out, "group", split_axis=0, concat_axis=0, tiled=True).reshape(
        cap_rows, feature_rows
    )
    mixing = jnp.sum(jnp.where(matches, routing_weights[None, :, :], 0.0), axis=2)
    mixed = jnp.einsum(
        "ct,cd->td", mixing, returned.astype(jnp.float32), precision=lax.Precision.HIGHEST
    )
    return mixed.astype(jnp.bfloat16)


def solution(mesh):
    return jax.shard_map(
        on_device,
        mesh=mesh,
        in_specs=(
            P(("dp", "group"), "local"),
            P(("dp", "group"), None),
            P(("dp", "group"), None),
            P(("dp", "group"), None),
            P("group", "local", None),
            P("group", "local", None),
            P("group", None, "local"),
        ),
        out_specs=P(("dp", "group"), "local"),
        check_vma=False,
    )
```

profile of v0, /device:TPU:24, one launch (start us, length us, event | category | flops | bytes accessed | tf_op | source)
XLA Modules:
  0.0 480.4 jit_solution(2588976456024908480)
XLA Ops:
  6.5 0.8 multiply_add_fusion
  7.4 0.1 fusion.15
  7.5 2.3 convolution_convert_fusion
  9.8 1.4 reshape.14
  11.2 166.6 %all_to_all.10 = bf16[32,18,896]{2,1,0:T(8,128)(2,1)} all-to-all(bf16[32,18,896]{2,1,0:T(8,128)(2,1)S(1)} %reshape.14), channel_id=1, replica_groups=mesh['group'=32,'local'=8,'dp'=4] {'group'}, dimensions={0} | all-to-all | bytes 2064384 | tf_op jit(solution)/shard_map/all_to_all | solution.py:20
  177.9 2.3 reshape.15
  180.1 2.6 fusion.6
  182.8 1.4 copy.14
  184.2 0.0 reduce-scatter.9.cloned.1.call-start
  184.3 3.2 fusion.9
  187.5 1.4 copy.16
  189.0 26.5 %reduce-scatter.7.cloned.1.call-done = bf16[128,576]{1,0:T(8,128)(2,1)} async-done(((bf16[1024,576]{1,0:T(8,128)(2,1)}), bf16[128,576]{1,0:T(8,128)(2,1)}) %reduce-scatter.7.cloned.1.call-update) | async-done | bytes 147472
  215.5 1.1 copy.15
  216.6 51.6 %reduce-scatter.9.cloned.1.call-done = bf16[128,576]{1,0:T(8,128)(2,1)} async-done(((bf16[1024,576]{1,0:T(8,128)(2,1)}), bf16[128,576]{1,0:T(8,128)(2,1)}) %reduce-scatter.9.cloned.1.call-update) | async-done | bytes 147472
  268.2 1.1 copy.17
  269.2 0.8 fusion.20
  270.0 41.6 %all-gather.2.cloned.1.call-done = bf16[576,1024]{1,0:T(8,128)(2,1)} async-done(((bf16[576,128]{1,0:T(8,128)(2,1)}), bf16[576,1024]{1,0:T(8,128)(2,1)}) %all-gather.2.cloned.1.call-update) | async-done | bytes 1179664 | tf_op jit(solution)/shard_map/all_gather | solution.py:36
  311.6 3.2 fusion.12
  314.9 1.3 reshape.16
  316.1 23.1 %all-to-all-start.1 = ((bf16[32,18,896]{2,1,0:T(8,128)(2,1)}), bf16[32,18,896]{2,1,0:T(8,128)(2,1)S(1)}, u32[]{:S(2)}, u32[]{:S(2)}) async-start(bf16[32,18,896]{2,1,0:T(8,128)(2,1)} %reshape.16), calls=%async_computation.1 | async-start | bytes 2752512 | tf_op jit(solution)/shard_map/all_to_all | solution.py:41
  339.2 0.1 select_reduce_fusion
  339.3 130.7 %all-to-all-done.1 = bf16[32,18,896]{2,1,0:T(8,128)(2,1)S(1)} async-done(((bf16[32,18,896]{2,1,0:T(8,128)(2,1)}), bf16[32,18,896]{2,1,0:T(8,128)(2,1)S(1)}, u32[]{:S(2)}, u32[]{:S(2)}) %all-to-all-start.1) | async-done | bytes 1032224 | tf_op jit(solution)/shard_map/all_to_all | solution.py:41
  470.0 1.1 reshape.17
  471.1 2.7 convolution_convert_fusion.1
  (9 shorter events, 0.1 us)
Async XLA Ops:
  6.5 173.6 %copy-start = (bf16[1,896,1024]{2,1,0:T(8,128)(2,1)S(1)}, bf16[1,896,1024]{2,1,0:T(8,128)(2,1)}, u32[]{:S(2)}) copy-start(bf16[1,896,1024]{2,1,0:T(8,128)(2,1)} %param.11) | copy-start | bytes 5505028
  6.5 209.0 %reduce-scatter.7.cloned.1.call-start = ((), (), s32[]{:S(2)}) async-start(), calls=%async_computation.5 | async-start | bytes 1474560
  184.2 83.9 %reduce-scatter.9.cloned.1.call-start = ((), (), s32[]{:S(2)}) async-start(), calls=%async_computation.6 | async-start | bytes 1474560
  189.0 122.7 %all-gather.2.cloned.1.call-start = ((), (), s32[]{:S(2)}) async-start(), calls=%async_computation.4 | async-start | bytes 1327104 | tf_op jit(solution)/shard_map/all_gather | solution.py:36
  316.1 23.1 %copy-start.1 = (f32[128,4]{0,1:T(4,128)S(1)}, f32[128,4]{0,1:T(4,128)}, u32[]{:S(2)}) copy-start(f32[128,4]{0,1:T(4,128)} %param.10) | copy-start | bytes 6148
  316.1 153.9 %all-to-all-start.1 = ((bf16[32,18,896]{2,1,0:T(8,128)(2,1)}), bf16[32,18,896]{2,1,0:T(8,128)(2,1)S(1)}, u32[]{:S(2)}, u32[]{:S(2)}) async-start(bf16[32,18,896]{2,1,0:T(8,128)(2,1)} %reshape.16), calls=%async_computation.1 | async-start | bytes 2752512 | tf_op jit(solution)/shard_map/all_to_all | solution.py:41
Sparse Core Ops, SparseCore 0:
  184.4 31.1 reduce-scatter.6
  218.9 49.1 reduce-scatter.8
  270.9 40.7 all-gather.1
where the time goes:
time: 482 us; the launch traced here: 480 us
  waiting for transfers between devices  250 us (52%)
  blocking collectives  167 us (35%)
  starting transfers between devices  23.1 us (5%)
  matrix products  14.1 us (3%)
  between operations  13.2 us (3%)
  local copies, waits for them, and re-layouts  11 us (2%)
    all_to_all x1, blocking collectives, on_device(): lax.all_to_all(outgoing, 'group', split_axis=0, concat_axis=0, tiled=True)  167 us
    all_to_all x1, waiting for transfers between devices, on_device(): lax.all_to_all(expert_out, 'group', split_axis=0, concat_axis=0, tiled=True)  131 us
    unnamed x5, waiting for transfers between devices  78.2 us
    all_gather x1, waiting for transfers between devices, on_device(): lax.all_gather(hidden_share, 'local', axis=1, tiled=True)  41.6 us
    all_to_all x1, starting transfers between devices, on_device(): lax.all_to_all(expert_out, 'group', split_axis=0, concat_axis=0, tiled=True)  23.1 us
  transfers between devices with their start and end apart: 4, of which 4 were waited for; matrix products, arithmetic and copies ran while one was open for 1% of the time, Pallas kernels for 0%

commit v1 on v0

v1 whole, which is shorter than its diff:
```python
import jax
import jax.numpy as jnp
from jax import lax
from jax.sharding import PartitionSpec as P

LANES = 128
BASE = 16


def on_device(tokens, group_ids, send_slots, routing_weights, gate_proj, up_proj, down_proj, n_chunks=2):
    f32, bf16 = jnp.float32, jnp.bfloat16
    groups = lax.axis_size("group")
    n_local = lax.axis_size("local")
    n_x = n_local // 2
    tok_rows, feats = tokens.shape
    hidden_size = gate_proj.shape[2]
    share = hidden_size // n_local
    half = hidden_size // 2
    where = lax.axis_index("local")
    core, at_x = where % 2, where // 2

    ids_t = group_ids.T
    group_iota = jnp.arange(groups, dtype=jnp.int32)
    named = ids_t[:, None, :] == group_iota[None, :, None]
    member = jnp.any(named, axis=0)
    weight_of = jnp.sum(jnp.where(named, routing_weights.T[:, None, :], 0.0), axis=0)
    before = jnp.arange(tok_rows)[:, None] < jnp.arange(tok_rows)[None, :]
    rank = jnp.dot(member.astype(bf16), before.astype(bf16), preferred_element_type=f32)
    rank = jnp.where(member, rank, -1.0).astype(jnp.int32)

    def rows_of(first, count):
        slots = first + jnp.arange(count, dtype=jnp.int32)
        match = rank[:, None, :] == slots[None, :, None]
        mixing = jnp.where(match, weight_of[:, None, :], 0.0)
        return match.reshape(groups * count, tok_rows), mixing.reshape(groups * count, tok_rows)

    def pick(match):
        return jnp.dot(match.astype(bf16), tokens, preferred_element_type=f32).astype(bf16)

    tiles = feats // LANES
    n_extra = 2
    extra_cols = -(-n_extra * tiles // 8)

    def pack(rows, per):
        a = rows.reshape(-1, n_extra * tiles, LANES)
        a = jnp.pad(a, ((0, 0), (0, per * ((n_extra * tiles + per - 1) // per) - n_extra * tiles), (0, 0)))
        k = a.shape[1] // per
        return a.reshape(-1, k, per, LANES).transpose(0, 2, 1, 3).reshape(-1, per, k * LANES)

    def unpack(block, per):
        k = block.shape[2] // LANES
        a = block.reshape(-1, per, k, LANES).transpose(0, 2, 1, 3).reshape(-1, k * per, LANES)
        return a[:, : n_extra * tiles].reshape(-1, feats)

    def order(w, axis, side):
        return [
            lax.dynamic_slice_in_dim(w, side * half + ((at_x + j) % n_x) * share, share, axis)
            for j in range(n_x)
        ]

    def both(side):
        cols = []
        for g, u in zip(order(gate_proj[0], 1, side), order(up_proj[0], 1, side)):
            cols += [g, u]
        return jnp.concatenate(cols, axis=1)

    w_other, w_mine = both(1 - core), both(core)
    d_mine = jnp.concatenate(order(down_proj[0], 0, core), axis=0)
    d_other = jnp.concatenate(order(down_proj[0], 0, 1 - core), axis=0)

    pair = [(i, i ^ 1) for i in range(n_local)]

    def x_shift(j):
        return [(i, ((i // 2 + j) % n_x) * 2 + i % 2) for i in range(n_local)]

    def a2a(v):
        return lax.all_to_all(v, "group", split_axis=0, concat_axis=0, tiled=True)

    def expert(arrived):
        other = jnp.dot(arrived, w_other, preferred_element_type=f32).astype(bf16)
        got = lax.ppermute(other, "local", pair)
        mine = jnp.dot(arrived, w_mine, preferred_element_type=f32).astype(bf16)
        total = mine.astype(f32) + got.astype(f32)
        width = 2 * share
        parts = [total[:, j * width : (j + 1) * width] for j in range(n_x)]
        came = [lax.ppermute(parts[j].astype(bf16), "local", x_shift(j)) for j in (2, 1, 3)]
        pre = parts[0] + sum(v.astype(f32) for v in came)
        hidden = (jax.nn.silu(pre[:, :share]) * pre[:, share:]).astype(bf16)
        shares = [hidden] + [None] * (n_x - 1)
        for j in (2, 1, 3):
            shares[j] = lax.ppermute(hidden, "local", x_shift(-j))
        hidden_mine = jnp.concatenate(shares, axis=1)
        hidden_other = lax.ppermute(hidden_mine, "local", pair)
        out = jnp.dot(hidden_mine, d_mine, preferred_element_type=f32) + jnp.dot(
            hidden_other, d_other, preferred_element_type=f32
        )
        return out.astype(bf16)

    per = BASE // n_chunks
    extra_match, extra_mixing = rows_of(BASE, n_extra)
    hot = jnp.any(rank >= BASE, axis=1)
    extra_rows = pick(jnp.any(extra_match.reshape(groups, n_extra, tok_rows), axis=0))
    extra_tile = pack(extra_rows, per)
    extra_send = jnp.where(hot[:, None, None], extra_tile, jnp.zeros((), bf16))

    arrivals = []
    mixings = []
    for k in range(n_chunks):
        match, mixing = rows_of(k * per, per)
        outgoing = pick(match).reshape(groups, per, feats)
        if k == n_chunks - 1:
            outgoing = jnp.concatenate([outgoing, extra_send], axis=2)
        arrivals.append(a2a(outgoing))
        mixings.append(mixing)

    mixed = None
    for k in range(n_chunks):
        got = arrivals[k]
        last = k == n_chunks - 1
        rows = got[:, :, :feats].reshape(groups * per, feats)
        if last:
            rows = jnp.concatenate([rows, unpack(got[:, :, feats:], per)], axis=0)
        out = expert(rows)
        back = out[: groups * per].reshape(groups, per, feats)
        if last:
            back = jnp.concatenate([back, pack(out[groups * per :], per)], axis=2)
        back = a2a(back)
        mixing = mixings[k]
        rows = back[:, :, :feats].reshape(groups * per, feats)
        if last:
            rows = jnp.concatenate([rows, unpack(back[:, :, feats:], per)], axis=0)
            mixing = jnp.concatenate([mixing, extra_mixing], axis=0)
        part = jnp.einsum("ct,cd->td", mixing, rows.astype(f32), precision=lax.Precision.HIGHEST)
        mixed = part if mixed is None else mixed + part
    return mixed.astype(bf16)


def solution(mesh):
    return jax.shard_map(
        on_device,
        mesh=mesh,
        in_specs=(
            P(("dp", "group"), "local"),
            P(("dp", "group"), None),
            P(("dp", "group"), None),
            P(("dp", "group"), None),
            P("group", "local", None),
            P("group", "local", None),
            P("group", None, "local"),
        ),
        out_specs=P(("dp", "group"), "local"),
        check_vma=False,
    )
```

time: 482 us -> 314 us (0.65)
  blocking collectives: 167 us -> 0 us
  starting transfers between devices: 23.1 us -> 90.5 us
  waiting for transfers between devices: 250 us -> 188 us
  between operations: 13.2 us -> 0.95 us
    all_to_all x1 -> x0, blocking collectives: 167 us -> none  [on_device(): lax.all_to_all(outgoing, 'group', split_axis=0, concat_axis=0, tiled=True)]
    unnamed x5 -> x0, waiting for transfers between devices: 78.2 us -> none
    ppermute x0 -> x16, starting transfers between devices: none -> 46.5 us  [the longest x6 19.7 us: expert(): lax.ppermute(parts[j].astype(bf16), 'local', x_shift(j))]
    all_gather x1 -> x0, waiting for transfers between devices: 41.6 us -> none  [on_device(): lax.all_gather(hidden_share, 'local', axis=1, tiled=True)]
    all_to_all x1 -> x4, waiting for transfers between devices: 131 us -> 164 us  [a2a(): return lax.all_to_all(v, 'group', split_axis=0, concat_axis=0, tiled=True)]
    ppermute x0 -> x16, waiting for transfers between devices: none -> 23.9 us  [the longest x6 11.9 us: expert(): lax.ppermute(parts[j].astype(bf16), 'local', x_shift(j))]
    all_to_all x1 -> x4, starting transfers between devices: 23.1 us -> 44 us  [a2a(): return lax.all_to_all(v, 'group', split_axis=0, concat_axis=0, tiled=True)]
    unnamed x8 -> x64, local copies, waits for them, and re-layouts: 4.99 us -> 11.8 us
  transfers between devices with their start and end apart: 4 -> 20, of which waited for: 4 -> 13; matrix products, arithmetic and copies ran while one was open for 1% -> 8% of each run, Pallas kernels for 0% -> 0%
where the time goes in v1:
time: 314 us; the launch traced here: 313 us
  waiting for transfers between devices  188 us (60%)
  starting transfers between devices  90.5 us (29%)
  local copies, waits for them, and re-layouts  15.4 us (5%)
  matrix products  15.3 us (5%)
  other arithmetic  3.19 us (1%)
    all_to_all x4, waiting for transfers between devices, a2a(): return lax.all_to_all(v, 'group', split_axis=0, concat_axis=0, tiled=True)  164 us
    all_to_all x4, starting transfers between devices, a2a(): return lax.all_to_all(v, 'group', split_axis=0, concat_axis=0, tiled=True)  44 us
    ppermute x6, starting transfers between devices, expert(): lax.ppermute(parts[j].astype(bf16), 'local', x_shift(j))  19.7 us
    ppermute x6, starting transfers between devices, expert(): shares[j] = lax.ppermute(hidden, 'local', x_shift(-j))  19 us
    ppermute x6, waiting for transfers between devices, expert(): lax.ppermute(parts[j].astype(bf16), 'local', x_shift(j))  11.9 us
    unnamed x64, local copies, waits for them, and re-layouts  11.8 us
    ppermute x6, waiting for transfers between devices, expert(): shares[j] = lax.ppermute(hidden, 'local', x_shift(-j))  8.05 us
  transfers between devices with their start and end apart: 20, of which 13 were waited for; matrix products, arithmetic and copies ran while one was open for 8% of the time, Pallas kernels for 0%

profile of v1, /device:TPU:24, one launch (start us, length us, event | category | flops | bytes accessed | tf_op | source)
XLA Modules:
  0.0 313.2 jit_solution(5597603581878114963)
XLA Ops:
  2.2 28.7 %all-to-all-start = ((bf16[32,8,896]{2,1,0:T(8,128)(2,1)}), bf16[32,8,896]{2,1,0:T(8,128)(2,1)S(1)}, u32[]{:S(2)}, u32[]{:S(2)}) async-start(bf16[32,8,896]{2,1,0:T(8,128)(2,1)} %fusion.5), calls=%async_computation | async-start | bytes 917504 | tf_op jit(solution)/shard_map/all_to_all | solution.py:77
  32.6 57.6 %all-to-all-done = bf16[32,8,896]{2,1,0:T(8,128)(2,1)S(1)} async-done(((bf16[32,8,896]{2,1,0:T(8,128)(2,1)}), bf16[32,8,896]{2,1,0:T(8,128)(2,1)S(1)}, u32[]{:S(2)}, u32[]{:S(2)}) %all-to-all-start) | async-done | bytes 458784 | tf_op jit(solution)/shard_map/all_to_all | solution.py:77
  90.2 3.9 %all-to-all-start.2 = ((bf16[32,8,1152]{2,1,0:T(8,128)(2,1)}), bf16[32,8,1152]{2,1,0:T(8,128)(2,1)S(1)}, u32[]{:S(2)}, u32[]{:S(2)}) async-start(bf16[32,8,1152]{2,1,0:T(8,128)(2,1)} %pad_maximum_fusion.2), calls=%async_computation.2 | async-start | bytes 1179648 | tf_op jit(solution)/shard_map/all_to_all | solution.py:77
  107.3 2.2 convolution_convert_fusion.2
  114.0 4.8 %collective-permute-start.3 = (bf16[256,256]{1,0:T(8,128)(2,1)S(1)}, bf16[256,256]{1,0:T(8,128)(2,1)S(1)}, u32[]{:S(2)}, u32[]{:S(2)}) collective-permute-start(bf16[256,256]{1,0:T(8,128)(2,1)S(1)} %get-tuple-element.25), channel_id=1, source_target_pairs={{0,24},{4,28},{8,0},{12,4},{16,8},{20,12},{24,16},{28,20},{1,25},{... | collective-permute-start | bytes 393224 | tf_op jit(solution)/shard_map/ppermute | solution.py:86
  120.8 4.2 %collective-permute-start.1 = (bf16[256,256]{1,0:T(8,128)(2,1)S(1)}, bf16[256,256]{1,0:T(8,128)(2,1)S(1)}, u32[]{:S(2)}, u32[]{:S(2)}) collective-permute-start(bf16[256,256]{1,0:T(8,128)(2,1)S(1)} %get-tuple-element.24), channel_id=1, source_target_pairs={{0,16},{4,20},{8,24},{12,28},{16,0},{20,4},{24,8},{28,12},{1,17},{... | collective-permute-start | bytes 393224 | tf_op jit(solution)/shard_map/ppermute | solution.py:86
  125.0 5.0 %collective-permute-done.2 = bf16[256,256]{1,0:T(8,128)(2,1)S(1)} collective-permute-done((bf16[256,256]{1,0:T(8,128)(2,1)S(1)}, bf16[256,256]{1,0:T(8,128)(2,1)S(1)}, u32[]{:S(2)}, u32[]{:S(2)}) %collective-permute-start.2) | collective-permute-done | bytes 131104 | tf_op jit(solution)/shard_map/ppermute | solution.py:86
  132.1 5.7 %collective-permute-start.5 = (bf16[256,128]{1,0:T(8,128)(2,1)S(1)}, bf16[256,128]{1,0:T(8,128)(2,1)S(1)}, u32[]{:S(2)}, u32[]{:S(2)}) collective-permute-start(bf16[256,128]{1,0:T(8,128)(2,1)S(1)} %fusion.23), channel_id=1, source_target_pairs={{0,16},{4,20},{8,24},{12,28},{16,0},{20,4},{24,8},{28,12},{1,17},{... | collective-permute-start | bytes 196616 | tf_op jit(solution)/shard_map/ppermute | solution.py:91
  137.8 2.1 collective-permute-start.4
  140.0 3.9 %collective-permute-done.4 = bf16[256,128]{1,0:T(8,128)(2,1)S(1)} collective-permute-done((bf16[256,128]{1,0:T(8,128)(2,1)S(1)}, bf16[256,128]{1,0:T(8,128)(2,1)S(1)}, u32[]{:S(2)}, u32[]{:S(2)}) %collective-permute-start.4) | collective-permute-done | bytes 65568 | tf_op jit(solution)/shard_map/ppermute | solution.py:91
  149.2 14.7 %all-to-all-done.2 = bf16[32,8,1152]{2,1,0:T(8,128)(2,1)S(1)} async-done(((bf16[32,8,1152]{2,1,0:T(8,128)(2,1)}), bf16[32,8,1152]{2,1,0:T(8,128)(2,1)S(1)}, u32[]{:S(2)}, u32[]{:S(2)}) %all-to-all-start.2) | async-done | bytes 589856 | tf_op jit(solution)/shard_map/all_to_all | solution.py:77
  164.2 3.3 %convolution_convert_fusion = bf16[320,1024]{1,0:T(8,128)(2,1)} fusion(bf16[896,1024]{1,0:T(8,128)(2,1)} %bitcast_dynamic-update-slice_fusion, bf16[64,896]{1,0:T(8,128)(2,1)S(1)} %reshape.118, bf16[256,896]{1,0:T(8,128)(2,1)S(1)} %slice_bitcast_fusion.2), kind=kOutput, calls=%fused_computation.1 | convolution fusion | flops 588677120 | bytes 3063808 | tf_op jit(solution)/shard_map/dot_general | solution.py:80
  170.7 7.5 %all-to-all-start.1 = ((bf16[32,8,896]{2,1,0:T(8,128)(2,1)}), bf16[32,8,896]{2,1,0:T(8,128)(2,1)S(1)}, u32[]{:S(2)}, u32[]{:S(2)}) async-start(bf16[32,8,896]{2,1,0:T(8,128)(2,1)} %fusion.4), calls=%async_computation.1 | async-start | bytes 917504 | tf_op jit(solution)/shard_map/all_to_all | solution.py:77
  180.3 3.5 %collective-permute-start.11 = (bf16[320,256]{1,0:T(8,128)(2,1)S(1)}, bf16[320,256]{1,0:T(8,128)(2,1)S(1)}, u32[]{:S(2)}, u32[]{:S(2)}) collective-permute-start(bf16[320,256]{1,0:T(8,128)(2,1)S(1)} %get-tuple-element.22), channel_id=1, source_target_pairs={{0,24},{4,28},{8,0},{12,4},{16,8},{20,12},{24,16},{28,20},{1,25},{... | collective-permute-start | bytes 491528 | tf_op jit(solution)/shard_map/ppermute | solution.py:86
  183.8 2.5 collective-permute-start.10
  186.3 2.8 collective-permute-start.9
  189.1 6.9 %collective-permute-done.10 = bf16[320,256]{1,0:T(8,128)(2,1)S(1)} collective-permute-done((bf16[320,256]{1,0:T(8,128)(2,1)S(1)}, bf16[320,256]{1,0:T(8,128)(2,1)S(1)}, u32[]{:S(2)}, u32[]{:S(2)}) %collective-permute-start.10) | collective-permute-done | bytes 163872 | tf_op jit(solution)/shard_map/ppermute | solution.py:86
  198.0 5.1 %collective-permute-start.13 = (bf16[320,128]{1,0:T(8,128)(2,1)S(1)}, bf16[320,128]{1,0:T(8,128)(2,1)S(1)}, u32[]{:S(2)}, u32[]{:S(2)}) collective-permute-start(bf16[320,128]{1,0:T(8,128)(2,1)S(1)} %fusion.17), channel_id=1, source_target_pairs={{0,16},{4,20},{8,24},{12,28},{16,0},{20,4},{24,8},{28,12},{1,17},{... | collective-permute-start | bytes 245768 | tf_op jit(solution)/shard_map/ppermute | solution.py:91
  203.1 2.3 collective-permute-start.12
  205.9 3.6 %collective-permute-done.12 = bf16[320,128]{1,0:T(8,128)(2,1)S(1)} collective-permute-done((bf16[320,128]{1,0:T(8,128)(2,1)S(1)}, bf16[320,128]{1,0:T(8,128)(2,1)S(1)}, u32[]{:S(2)}, u32[]{:S(2)}) %collective-permute-start.12) | collective-permute-done | bytes 81952 | tf_op jit(solution)/shard_map/ppermute | solution.py:91
  209.5 2.1 collective-permute-start.15
  215.3 22.4 %all-to-all-done.1 = bf16[32,8,896]{2,1,0:T(8,128)(2,1)S(1)} async-done(((bf16[32,8,896]{2,1,0:T(8,128)(2,1)}), bf16[32,8,896]{2,1,0:T(8,128)(2,1)S(1)}, u32[]{:S(2)}, u32[]{:S(2)}) %all-to-all-start.1) | async-done | bytes 458784 | tf_op jit(solution)/shard_map/all_to_all | solution.py:77
  237.7 3.9 %all-to-all-start.3 = ((bf16[32,8,1152]{2,1,0:T(8,128)(2,1)}), bf16[32,8,1152]{2,1,0:T(8,128)(2,1)S(1)}, u32[]{:S(2)}, u32[]{:S(2)}) async-start(bf16[32,8,1152]{2,1,0:T(8,128)(2,1)} %pad_maximum_fusion.3), calls=%async_computation.3 | async-start | bytes 1179648 | tf_op jit(solution)/shard_map/all_to_all | solution.py:77
  242.4 69.2 %all-to-all-done.3 = bf16[32,8,1152]{2,1,0:T(8,128)(2,1)S(1)} async-done(((bf16[32,8,1152]{2,1,0:T(8,128)(2,1)}), bf16[32,8,1152]{2,1,0:T(8,128)(2,1)S(1)}, u32[]{:S(2)}, u32[]{:S(2)}) %all-to-all-start.3) | async-done | bytes 589856 | tf_op jit(solution)/shard_map/all_to_all | solution.py:77
  (135 shorter events, 44.4 us)
Async XLA Ops:
  2.2 88.0 %all-to-all-start = ((bf16[32,8,896]{2,1,0:T(8,128)(2,1)}), bf16[32,8,896]{2,1,0:T(8,128)(2,1)S(1)}, u32[]{:S(2)}, u32[]{:S(2)}) async-start(bf16[32,8,896]{2,1,0:T(8,128)(2,1)} %fusion.5), calls=%async_computation | async-start | bytes 917504 | tf_op jit(solution)/shard_map/all_to_all | solution.py:77
  90.2 73.7 %all-to-all-start.2 = ((bf16[32,8,1152]{2,1,0:T(8,128)(2,1)}), bf16[32,8,1152]{2,1,0:T(8,128)(2,1)S(1)}, u32[]{:S(2)}, u32[]{:S(2)}) async-start(bf16[32,8,1152]{2,1,0:T(8,128)(2,1)} %pad_maximum_fusion.2), calls=%async_computation.2 | async-start | bytes 1179648 | tf_op jit(solution)/shard_map/all_to_all | solution.py:77
  109.5 3.8 %collective-permute-start = (bf16[256,1024]{1,0:T(8,128)(2,1)S(1)}, bf16[256,1024]{1,0:T(8,128)(2,1)S(1)}, u32[]{:S(2)}, u32[]{:S(2)}) collective-permute-start(bf16[256,1024]{1,0:T(8,128)(2,1)S(1)} %convolution_convert_fusion.2), channel_id=1, source_target_pairs={{0,4},{4,0},{8,12},{12,8},{16,20},{20,16},{24,28},{28,24},{1,5},{5... | collective-permute-start | bytes 1572872 | tf_op jit(solution)/shard_map/ppermute | solution.py:81
  114.0 10.9 %collective-permute-start.3 = (bf16[256,256]{1,0:T(8,128)(2,1)S(1)}, bf16[256,256]{1,0:T(8,128)(2,1)S(1)}, u32[]{:S(2)}, u32[]{:S(2)}) collective-permute-start(bf16[256,256]{1,0:T(8,128)(2,1)S(1)} %get-tuple-element.25), channel_id=1, source_target_pairs={{0,24},{4,28},{8,0},{12,4},{16,8},{20,12},{24,16},{28,20},{1,25},{... | collective-permute-start | bytes 393224 | tf_op jit(solution)/shard_map/ppermute | solution.py:86
  118.8 11.2 %collective-permute-start.2 = (bf16[256,256]{1,0:T(8,128)(2,1)S(1)}, bf16[256,256]{1,0:T(8,128)(2,1)S(1)}, u32[]{:S(2)}, u32[]{:S(2)}) collective-permute-start(bf16[256,256]{1,0:T(8,128)(2,1)S(1)} %get-tuple-element.26), channel_id=1, source_target_pairs={{0,8},{4,12},{8,16},{12,20},{16,24},{20,28},{24,0},{28,4},{1,9},{5... | collective-permute-start | bytes 393224 | tf_op jit(solution)/shard_map/ppermute | solution.py:86
  120.8 9.2 %collective-permute-start.1 = (bf16[256,256]{1,0:T(8,128)(2,1)S(1)}, bf16[256,256]{1,0:T(8,128)(2,1)S(1)}, u32[]{:S(2)}, u32[]{:S(2)}) collective-permute-start(bf16[256,256]{1,0:T(8,128)(2,1)S(1)} %get-tuple-element.24), channel_id=1, source_target_pairs={{0,16},{4,20},{8,24},{12,28},{16,0},{20,4},{24,8},{28,12},{1,17},{... | collective-permute-start | bytes 393224 | tf_op jit(solution)/shard_map/ppermute | solution.py:86
  130.1 9.8 %collective-permute-start.6 = (bf16[256,128]{1,0:T(8,128)(2,1)S(1)}, bf16[256,128]{1,0:T(8,128)(2,1)S(1)}, u32[]{:S(2)}, u32[]{:S(2)}) collective-permute-start(bf16[256,128]{1,0:T(8,128)(2,1)S(1)} %fusion.23), channel_id=1, source_target_pairs={{0,8},{4,12},{8,16},{12,20},{16,24},{20,28},{24,0},{28,4},{1,9},{5... | collective-permute-start | bytes 196616 | tf_op jit(solution)/shard_map/ppermute | solution.py:91
  132.1 7.9 %collective-permute-start.5 = (bf16[256,128]{1,0:T(8,128)(2,1)S(1)}, bf16[256,128]{1,0:T(8,128)(2,1)S(1)}, u32[]{:S(2)}, u32[]{:S(2)}) collective-permute-start(bf16[256,128]{1,0:T(8,128)(2,1)S(1)} %fusion.23), channel_id=1, source_target_pairs={{0,16},{4,20},{8,24},{12,28},{16,0},{20,4},{24,8},{28,12},{1,17},{... | collective-permute-start | bytes 196616 | tf_op jit(solution)/shard_map/ppermute | solution.py:91
  137.8 6.2 %collective-permute-start.4 = (bf16[256,128]{1,0:T(8,128)(2,1)S(1)}, bf16[256,128]{1,0:T(8,128)(2,1)S(1)}, u32[]{:S(2)}, u32[]{:S(2)}) collective-permute-start(bf16[256,128]{1,0:T(8,128)(2,1)S(1)} %fusion.23), channel_id=1, source_target_pairs={{0,24},{4,28},{8,0},{12,4},{16,8},{20,12},{24,16},{28,20},{1,25},{... | collective-permute-start | bytes 196616 | tf_op jit(solution)/shard_map/ppermute | solution.py:91
  144.0 3.4 %collective-permute-start.7 = (bf16[256,512]{1,0:T(8,128)(2,1)S(1)}, bf16[256,512]{1,0:T(8,128)(2,1)S(1)}, u32[]{:S(2)}, u32[]{:S(2)}) collective-permute-start(bf16[256,512]{1,0:T(8,128)(2,1)S(1)} %pad_maximum_fusion.10), channel_id=1, source_target_pairs={{0,4},{4,0},{8,12},{12,8},{16,20},{20,16},{24,28},{28,24},{1,5},{5... | collective-permute-start | bytes 786440 | tf_op jit(solution)/shard_map/ppermute | solution.py:93
  167.5 10.7 %collective-permute-start.8 = (bf16[320,1024]{1,0:T(8,128)(2,1)}, bf16[320,1024]{1,0:T(8,128)(2,1)}, u32[]{:S(2)}, u32[]{:S(2)}) collective-permute-start(bf16[320,1024]{1,0:T(8,128)(2,1)} %convolution_convert_fusion), channel_id=1, source_target_pairs={{0,4},{4,0},{8,12},{12,8},{16,20},{20,16},{24,28},{28,24},{1,5},{5... | collective-permute-start | bytes 1966088 | tf_op jit(solution)/shard_map/ppermute | solution.py:81
  170.7 67.0 %all-to-all-start.1 = ((bf16[32,8,896]{2,1,0:T(8,128)(2,1)}), bf16[32,8,896]{2,1,0:T(8,128)(2,1)S(1)}, u32[]{:S(2)}, u32[]{:S(2)}) async-start(bf16[32,8,896]{2,1,0:T(8,128)(2,1)} %fusion.4), calls=%async_computation.1 | async-start | bytes 917504 | tf_op jit(solution)/shard_map/all_to_all | solution.py:77
  180.2 32.9 %copy-start.11 = (bf16[128,896]{1,0:T(8,128)(2,1)S(1)}, bf16[128,896]{1,0:T(8,128)(2,1)}, u32[]{:S(2)}) copy-start(bf16[128,896]{1,0:T(8,128)(2,1)} %copy-done.10) | copy-start | bytes 688132
  180.2 32.9 %copy-start.13 = (bf16[128,896]{1,0:T(8,128)(2,1)S(1)}, bf16[128,896]{1,0:T(8,128)(2,1)}, u32[]{:S(2)}) copy-start(bf16[128,896]{1,0:T(8,128)(2,1)} %copy-done.12) | copy-start | bytes 688132
  180.2 32.9 %copy-start.15 = (bf16[128,896]{1,0:T(8,128)(2,1)S(1)}, bf16[128,896]{1,0:T(8,128)(2,1)}, u32[]{:S(2)}) copy-start(bf16[128,896]{1,0:T(8,128)(2,1)} %copy-done.14) | copy-start | bytes 688132
  180.2 32.9 %copy-start.17 = (bf16[128,896]{1,0:T(8,128)(2,1)S(1)}, bf16[128,896]{1,0:T(8,128)(2,1)}, u32[]{:S(2)}) copy-start(bf16[128,896]{1,0:T(8,128)(2,1)} %copy-done.16) | copy-start | bytes 688132
  180.3 8.8 %collective-permute-start.11 = (bf16[320,256]{1,0:T(8,128)(2,1)S(1)}, bf16[320,256]{1,0:T(8,128)(2,1)S(1)}, u32[]{:S(2)}, u32[]{:S(2)}) collective-permute-start(bf16[320,256]{1,0:T(8,128)(2,1)S(1)} %get-tuple-element.22), channel_id=1, source_target_pairs={{0,24},{4,28},{8,0},{12,4},{16,8},{20,12},{24,16},{28,20},{1,25},{... | collective-permute-start | bytes 491528 | tf_op jit(solution)/shard_map/ppermute | solution.py:86
  183.8 12.2 %collective-permute-start.10 = (bf16[320,256]{1,0:T(8,128)(2,1)S(1)}, bf16[320,256]{1,0:T(8,128)(2,1)S(1)}, u32[]{:S(2)}, u32[]{:S(2)}) collective-permute-start(bf16[320,256]{1,0:T(8,128)(2,1)S(1)} %get-tuple-element.23), channel_id=1, source_target_pairs={{0,8},{4,12},{8,16},{12,20},{16,24},{20,28},{24,0},{28,4},{1,9},{5... | collective-permute-start | bytes 491528 | tf_op jit(solution)/shard_map/ppermute | solution.py:86
  186.3 9.7 %collective-permute-start.9 = (bf16[320,256]{1,0:T(8,128)(2,1)S(1)}, bf16[320,256]{1,0:T(8,128)(2,1)S(1)}, u32[]{:S(2)}, u32[]{:S(2)}) collective-permute-start(bf16[320,256]{1,0:T(8,128)(2,1)S(1)} %get-tuple-element.21), channel_id=1, source_target_pairs={{0,16},{4,20},{8,24},{12,28},{16,0},{20,4},{24,8},{28,12},{1,17},{... | collective-permute-start | bytes 491528 | tf_op jit(solution)/shard_map/ppermute | solution.py:86
  196.1 9.3 %collective-permute-start.14 = (bf16[320,128]{1,0:T(8,128)(2,1)S(1)}, bf16[320,128]{1,0:T(8,128)(2,1)S(1)}, u32[]{:S(2)}, u32[]{:S(2)}) collective-permute-start(bf16[320,128]{1,0:T(8,128)(2,1)S(1)} %fusion.17), channel_id=1, source_target_pairs={{0,8},{4,12},{8,16},{12,20},{16,24},{20,28},{24,0},{28,4},{1,9},{5... | collective-permute-start | bytes 245768 | tf_op jit(solution)/shard_map/ppermute | solution.py:91
  198.0 7.8 %collective-permute-start.13 = (bf16[320,128]{1,0:T(8,128)(2,1)S(1)}, bf16[320,128]{1,0:T(8,128)(2,1)S(1)}, u32[]{:S(2)}, u32[]{:S(2)}) collective-permute-start(bf16[320,128]{1,0:T(8,128)(2,1)S(1)} %fusion.17), channel_id=1, source_target_pairs={{0,16},{4,20},{8,24},{12,28},{16,0},{20,4},{24,8},{28,12},{1,17},{... | collective-permute-start | bytes 245768 | tf_op jit(solution)/shard_map/ppermute | solution.py:91
  203.1 6.3 %collective-permute-start.12 = (bf16[320,128]{1,0:T(8,128)(2,1)S(1)}, bf16[320,128]{1,0:T(8,128)(2,1)S(1)}, u32[]{:S(2)}, u32[]{:S(2)}) collective-permute-start(bf16[320,128]{1,0:T(8,128)(2,1)S(1)} %fusion.17), channel_id=1, source_target_pairs={{0,24},{4,28},{8,0},{12,4},{16,8},{20,12},{24,16},{28,20},{1,25},{... | collective-permute-start | bytes 245768 | tf_op jit(solution)/shard_map/ppermute | solution.py:91
  209.5 3.7 %collective-permute-start.15 = (bf16[320,512]{1,0:T(8,128)(2,1)S(1)}, bf16[320,512]{1,0:T(8,128)(2,1)S(1)}, u32[]{:S(2)}, u32[]{:S(2)}) collective-permute-start(bf16[320,512]{1,0:T(8,128)(2,1)S(1)} %pad_maximum_fusion.9), channel_id=1, source_target_pairs={{0,4},{4,0},{8,12},{12,8},{16,20},{20,16},{24,28},{28,24},{1,5},{5... | collective-permute-start | bytes 983048 | tf_op jit(solution)/shard_map/ppermute | solution.py:93
  237.7 73.9 %all-to-all-start.3 = ((bf16[32,8,1152]{2,1,0:T(8,128)(2,1)}), bf16[32,8,1152]{2,1,0:T(8,128)(2,1)S(1)}, u32[]{:S(2)}, u32[]{:S(2)}) async-start(bf16[32,8,1152]{2,1,0:T(8,128)(2,1)} %pad_maximum_fusion.3), calls=%async_computation.3 | async-start | bytes 1179648 | tf_op jit(solution)/shard_map/all_to_all | solution.py:77
  (23 other events, 172.2 us)

commit v2 on v1

--- a/solution.py
+++ b/solution.py
@@ -7,7 +7,7 @@
 BASE = 16
 
 
-def on_device(tokens, group_ids, send_slots, routing_weights, gate_proj, up_proj, down_proj, n_chunks=2):
+def on_device(tokens, group_ids, send_slots, routing_weights, gate_proj, up_proj, down_proj, n_chunks=1):
     f32, bf16 = jnp.float32, jnp.bfloat16
     groups = lax.axis_size("group")
     n_local = lax.axis_size("local")
@@ -17,7 +17,7 @@
     share = hidden_size // n_local
     half = hidden_size // 2
     where = lax.axis_index("local")
-    core, at_x = where % 2, where // 2
+    core = where % 2
 
     ids_t = group_ids.T
     group_iota = jnp.arange(groups, dtype=jnp.int32)
@@ -54,7 +54,7 @@
 
     def order(w, axis, side):
         return [
-            lax.dynamic_slice_in_dim(w, side * half + ((at_x + j) % n_x) * share, share, axis)
+            lax.dynamic_slice_in_dim(w, side * half + j * share, share, axis)
             for j in range(n_x)
         ]
 
@@ -70,8 +70,10 @@
 
     pair = [(i, i ^ 1) for i in range(n_local)]
 
-    def x_shift(j):
-        return [(i, ((i // 2 + j) % n_x) * 2 + i % 2) for i in range(n_local)]
+    rings = [[2 * i + c for i in range(n_x)] for c in range(2)]
+
+    def x_all(v):
+        return lax.all_to_all(v, "local", split_axis=0, concat_axis=0, tiled=True, axis_index_groups=rings)
 
     def a2a(v):
         return lax.all_to_all(v, "group", split_axis=0, concat_axis=0, tiled=True)
@@ -82,19 +84,26 @@
         mine = jnp.dot(arrived, w_mine, preferred_element_type=f32).astype(bf16)
         total = mine.astype(f32) + got.astype(f32)
         width = 2 * share
-        parts = [total[:, j * width : (j + 1) * width] for j in range(n_x)]
-        came = [lax.ppermute(parts[j].astype(bf16), "local", x_shift(j)) for j in (2, 1, 3)]
-        pre = parts[0] + sum(v.astype(f32) for v in came)
+        parts = jnp.stack([total[:, j * width : (j + 1) * width] for j in range(n_x)])
+        pre = jnp.sum(x_all(parts.astype(bf16)).astype(f32), axis=0)
         hidden = (jax.nn.silu(pre[:, :share]) * pre[:, share:]).astype(bf16)
-        shares = [hidden] + [None] * (n_x - 1)
-        for j in (2, 1, 3):
-            shares[j] = lax.ppermute(hidden, "local", x_shift(-j))
-        hidden_mine = jnp.concatenate(shares, axis=1)
+        shares = x_all(jnp.broadcast_to(hidden[None], (n_x,) + hidden.shape))
+        hidden_mine = jnp.concatenate([shares[j] for j in range(n_x)], axis=1)
         hidden_other = lax.ppermute(hidden_mine, "local", pair)
         out = jnp.dot(hidden_mine, d_mine, preferred_element_type=f32) + jnp.dot(
             hidden_other, d_other, preferred_element_type=f32
         )
         return out.astype(bf16)
+
+    def mix(mixing, rows):
+        out = None
+        left = mixing
+        for _ in range(3):
+            term = lax.reduce_precision(left, 8, 7)
+            left = left - term
+            part = jnp.einsum("ct,cd->td", term.astype(bf16), rows, preferred_element_type=f32)
+            out = part if out is None else out + part
+        return out
 
     per = BASE // n_chunks
     extra_match, extra_mixing = rows_of(BASE, n_extra)
@@ -113,24 +122,31 @@
         arrivals.append(a2a(outgoing))
         mixings.append(mixing)
 
-    mixed = None
+    returned = []
+    sent = None
     for k in range(n_chunks):
         got = arrivals[k]
         last = k == n_chunks - 1
+        if sent is not None:
+            got, sent = lax.optimization_barrier((got, sent))
+            returned.append(a2a(sent))
         rows = got[:, :, :feats].reshape(groups * per, feats)
         if last:
             rows = jnp.concatenate([rows, unpack(got[:, :, feats:], per)], axis=0)
         out = expert(rows)
-        back = out[: groups * per].reshape(groups, per, feats)
+        sent = out[: groups * per].reshape(groups, per, feats)
         if last:
-            back = jnp.concatenate([back, pack(out[groups * per :], per)], axis=2)
-        back = a2a(back)
-        mixing = mixings[k]
+            sent = jnp.concatenate([sent, pack(out[groups * per :], per)], axis=2)
+    returned.append(a2a(sent))
+
+    mixed = None
+    for k in range(n_chunks):
+        back, mixing = returned[k], mixings[k]
         rows = back[:, :, :feats].reshape(groups * per, feats)
-        if last:
+        if k == n_chunks - 1:
             rows = jnp.concatenate([rows, unpack(back[:, :, feats:], per)], axis=0)
             mixing = jnp.concatenate([mixing, extra_mixing], axis=0)
-        part = jnp.einsum("ct,cd->td", mixing, rows.astype(f32), precision=lax.Precision.HIGHEST)
+        part = mix(mixing, rows)
         mixed = part if mixed is None else mixed + part
     return mixed.astype(bf16)
 

time: 314 us -> 302 us (0.962)
  starting transfers between devices: 90.5 us -> 40 us
  blocking collectives: 0 us -> 32.7 us
  waiting for transfers between devices: 188 us -> 205 us
  matrix products: 15.3 us -> 8.68 us
  local copies, waits for them, and re-layouts: 15.4 us -> 10.5 us
    ppermute x12 -> x0, starting transfers between devices: 38.7 us -> none  [the longest x6 19.7 us: expert(): lax.ppermute(parts[j].astype(bf16), 'local', x_shift(j))]
    all_to_all x4 -> x2, waiting for transfers between devices: 164 us -> 201 us  [a2a(): return lax.all_to_all(v, 'group', split_axis=0, concat_axis=0, tiled=True)]
    all_to_all x0 -> x2, blocking collectives: none -> 32.7 us  [x_all(): lax.all_to_all(v, 'local', split_axis=0, concat_axis=0, tiled=True, axis_...]
    ppermute x12 -> x0, waiting for transfers between devices: 20 us -> none  [the longest x6 11.9 us: expert(): lax.ppermute(parts[j].astype(bf16), 'local', x_shift(j))]
    all_to_all x4 -> x2, starting transfers between devices: 44 us -> 36.1 us  [a2a(): return lax.all_to_all(v, 'group', split_axis=0, concat_axis=0, tiled=True)]
    unnamed x64 -> x26, local copies, waits for them, and re-layouts: 11.8 us -> 7.48 us
  transfers between devices with their start and end apart: 20 -> 4, of which waited for: 13 -> 4; matrix products, arithmetic and copies ran while one was open for 8% -> 3% of each run, Pallas kernels for 0% -> 0%
where the time goes in v2:
time: 302 us; the launch traced here: 301 us
  waiting for transfers between devices  205 us (68%)
  starting transfers between devices  40 us (13%)
  blocking collectives  32.7 us (11%)
  local copies, waits for them, and re-layouts  10.5 us (3%)
  matrix products  8.68 us (3%)
  other arithmetic  4.01 us (1%)
    all_to_all x2, waiting for transfers between devices, a2a(): return lax.all_to_all(v, 'group', split_axis=0, concat_axis=0, tiled=True)  201 us
    all_to_all x2, starting transfers between devices, a2a(): return lax.all_to_all(v, 'group', split_axis=0, concat_axis=0, tiled=True)  36.1 us
    all_to_all x2, blocking collectives, x_all(): lax.all_to_all(v, 'local', split_axis=0, concat_axis=0, tiled=True, axis_...  32.7 us
    unnamed x26, local copies, waits for them, and re-layouts  7.48 us
  transfers between devices with their start and end apart: 4, of which 4 were waited for; matrix products, arithmetic and copies ran while one was open for 3% of the time, Pallas kernels for 0%

profile of v2, /device:TPU:24, one launch (start us, length us, event | category | flops | bytes accessed | tf_op | source)
XLA Modules:
  0.0 300.9 jit_solution(5658451446692070759)
XLA Ops:
  2.0 1.1 pad_maximum_fusion.1
  3.2 28.7 %all-to-all-start = ((bf16[32,16,1024]{2,1,0:T(8,128)(2,1)}), bf16[32,16,1024]{2,1,0:T(8,128)(2,1)S(1)}, u32[]{:S(2)}, u32[]{:S(2)}) async-start(bf16[32,16,1024]{2,1,0:T(8,128)(2,1)} %pad_maximum_fusion.1), calls=%async_computation | async-start | bytes 2097152 | tf_op jit(solution)/shard_map/all_to_all | solution.py:79
  32.1 1.1 bitcast_dynamic-update-slice_fusion.14
  33.3 1.0 bitcast_dynamic-update-slice_fusion.12
  34.3 0.9 bitcast_dynamic-update-slice_fusion.11
  35.3 0.9 bitcast_dynamic-update-slice_fusion.10
  36.1 0.9 bitcast_dynamic-update-slice_fusion.9
  37.0 0.9 bitcast_dynamic-update-slice_fusion.8
  37.9 0.9 bitcast_dynamic-update-slice_fusion.3
  38.8 0.8 bitcast_dynamic-update-slice_fusion.2
  40.3 0.8 bitcast_dynamic-update-slice_fusion
  41.2 95.8 %all-to-all-done = bf16[32,16,1024]{2,1,0:T(8,128)(2,1)S(1)} async-done(((bf16[32,16,1024]{2,1,0:T(8,128)(2,1)}), bf16[32,16,1024]{2,1,0:T(8,128)(2,1)S(1)}, u32[]{:S(2)}, u32[]{:S(2)}) %all-to-all-start) | async-done | bytes 1048608 | tf_op jit(solution)/shard_map/all_to_all | solution.py:79
  137.3 3.1 %convolution_convert_fusion = bf16[576,1024]{1,0:T(8,128)(2,1)S(1)} fusion(bf16[896,1024]{1,0:T(8,128)(2,1)} %bitcast_dynamic-update-slice_fusion, bf16[64,896]{1,0:T(8,128)(2,1)S(1)} %reshape.72, bf16[512,896]{1,0:T(8,128)(2,1)S(1)} %bitcast.93), kind=kOutput, calls=%fused_computation.5 | convolution fusion | flops 1059618816 | bytes 4046848 | tf_op jit(solution)/shard_map/dot_general | solution.py:82
  140.3 1.9 collective-permute-start
  142.3 2.8 collective-permute-done
  145.1 1.4 add_convert_fusion
  146.7 20.9 %all_to_all.20 = bf16[4,576,256]{2,1,0:T(8,128)(2,1)S(1)} all-to-all(bf16[4,576,256]{2,1,0:T(8,128)(2,1)S(1)} %pad_maximum_fusion), channel_id=1, replica_groups={{0,8,16,24},{4,12,20,28},{1,9,17,25},{5,13,21,29},{2,10,18,26},{6,14,22..., dimensions={0} | all-to-all | bytes 2359296 | tf_op jit(solution)/shard_map/all_to_all | solution.py:76
  168.0 11.8 %all_to_all.21 = bf16[4,576,128]{2,1,0:T(8,128)(2,1)S(1)} all-to-all(bf16[4,576,128]{2,1,0:T(8,128)(2,1)S(1)} %broadcast_in_dim.97), channel_id=1, replica_groups={{0,8,16,24},{4,12,20,28},{1,9,17,25},{5,13,21,29},{2,10,18,26},{6,14,22..., dimensions={0} | all-to-all | bytes 1179648 | tf_op jit(solution)/shard_map/all_to_all | solution.py:76
  179.9 1.9 collective-permute-start.1
  182.8 1.0 collective-permute-done.1
  184.9 1.1 fusion.3
  186.0 7.4 %all-to-all-start.3 = ((bf16[32,16,1024]{2,1,0:T(8,128)(2,1)}), bf16[32,16,1024]{2,1,0:T(8,128)(2,1)S(1)}, u32[]{:S(2)}, u32[]{:S(2)}) async-start(bf16[32,16,1024]{2,1,0:T(8,128)(2,1)} %fusion.3), calls=%async_computation.3 | async-start | bytes 2097152 | tf_op jit(solution)/shard_map/all_to_all | solution.py:79
  193.8 104.9 %all-to-all-done.3 = bf16[32,16,1024]{2,1,0:T(8,128)(2,1)S(1)} async-done(((bf16[32,16,1024]{2,1,0:T(8,128)(2,1)}), bf16[32,16,1024]{2,1,0:T(8,128)(2,1)S(1)}, u32[]{:S(2)}, u32[]{:S(2)}) %all-to-all-start.3) | async-done | bytes 1048608 | tf_op jit(solution)/shard_map/all_to_all | solution.py:79
  299.8 1.1 fusion.1
  (59 shorter events, 7.2 us)
Async XLA Ops:
  0.0 1.1 copy-start
  2.0 29.9 %copy-start.1 = (bf16[1,896,1024]{2,1,0:T(8,128)(2,1)S(1)}, bf16[1,896,1024]{2,1,0:T(8,128)(2,1)}, u32[]{:S(2)}) copy-start(bf16[1,896,1024]{2,1,0:T(8,128)(2,1)} %param.10) | copy-start | bytes 5505028
  3.2 133.8 %all-to-all-start = ((bf16[32,16,1024]{2,1,0:T(8,128)(2,1)}), bf16[32,16,1024]{2,1,0:T(8,128)(2,1)S(1)}, u32[]{:S(2)}, u32[]{:S(2)}) async-start(bf16[32,16,1024]{2,1,0:T(8,128)(2,1)} %pad_maximum_fusion.1), calls=%async_computation | async-start | bytes 2097152 | tf_op jit(solution)/shard_map/all_to_all | solution.py:79
  32.0 3.3 %copy-start.2 = (bf16[1,896,1024]{2,1,0:T(8,128)(2,1)S(1)}, bf16[1,896,1024]{2,1,0:T(8,128)(2,1)}, u32[]{:S(2)}) copy-start(bf16[1,896,1024]{2,1,0:T(8,128)(2,1)} %param.11) | copy-start | bytes 5505028
  37.9 2.4 copy-start.4
  137.3 7.8 %copy-start.5 = (bf16[896,1024]{1,0:T(8,128)(2,1)S(1)}, bf16[896,1024]{1,0:T(8,128)(2,1)}, u32[]{:S(2)}) copy-start(bf16[896,1024]{1,0:T(8,128)(2,1)} %copy-done.4) | copy-start | bytes 5505028
  140.3 4.7 %collective-permute-start = (bf16[576,1024]{1,0:T(8,128)(2,1)S(1)}, bf16[576,1024]{1,0:T(8,128)(2,1)S(1)}, u32[]{:S(2)}, u32[]{:S(2)}) collective-permute-start(bf16[576,1024]{1,0:T(8,128)(2,1)S(1)} %convolution_convert_fusion), channel_id=1, source_target_pairs={{0,4},{4,0},{8,12},{12,8},{16,20},{20,16},{24,28},{28,24},{1,5},{5... | collective-permute-start | bytes 3538952 | tf_op jit(solution)/shard_map/ppermute | solution.py:83
  168.0 13.9 %copy-start.3 = (bf16[1,1024,896]{2,1,0:T(8,128)(2,1)S(1)}, bf16[1,1024,896]{2,1,0:T(8,128)(2,1)}, u32[]{:S(2)}) copy-start(bf16[1,1024,896]{2,1,0:T(8,128)(2,1)} %param.12) | copy-start | bytes 5505028
  179.9 3.9 %collective-permute-start.1 = (bf16[576,512]{1,0:T(8,128)(2,1)S(1)}, bf16[576,512]{1,0:T(8,128)(2,1)S(1)}, u32[]{:S(2)}, u32[]{:S(2)}) collective-permute-start(bf16[576,512]{1,0:T(8,128)(2,1)S(1)} %pad_maximum_fusion.6), channel_id=1, source_target_pairs={{0,4},{4,0},{8,12},{12,8},{16,20},{20,16},{24,28},{28,24},{1,5},{5... | collective-permute-start | bytes 1769480 | tf_op jit(solution)/shard_map/ppermute | solution.py:92
  184.9 8.5 %copy-start.6 = (s32[128,4]{0,1:T(4,128)S(1)}, s32[128,4]{0,1:T(4,128)}, u32[]{:S(2)}) copy-start(s32[128,4]{0,1:T(4,128)} %param.8) | copy-start | bytes 6148
  184.9 8.5 %copy-start.7 = (f32[128,4]{0,1:T(4,128)S(1)}, f32[128,4]{0,1:T(4,128)}, u32[]{:S(2)}) copy-start(f32[128,4]{0,1:T(4,128)} %param.9) | copy-start | bytes 6148
  186.0 112.7 %all-to-all-start.3 = ((bf16[32,16,1024]{2,1,0:T(8,128)(2,1)}), bf16[32,16,1024]{2,1,0:T(8,128)(2,1)S(1)}, u32[]{:S(2)}, u32[]{:S(2)}) async-start(bf16[32,16,1024]{2,1,0:T(8,128)(2,1)} %fusion.3), calls=%async_computation.3 | async-start | bytes 2097152 | tf_op jit(solution)/shard_map/all_to_all | solution.py:79

commit v3 on v2

--- a/solution.py
+++ b/solution.py
@@ -20,7 +20,8 @@
     core = where % 2
 
     ids_t = group_ids.T
-    group_iota = jnp.arange(groups, dtype=jnp.int32)
+    peers = [i // 2 + (i % 2) * (groups // 2) for i in range(groups)]
+    group_iota = jnp.array(peers, dtype=jnp.int32)
     named = ids_t[:, None, :] == group_iota[None, :, None]
     member = jnp.any(named, axis=0)
     weight_of = jnp.sum(jnp.where(named, routing_weights.T[:, None, :], 0.0), axis=0)
@@ -76,7 +77,7 @@
         return lax.all_to_all(v, "local", split_axis=0, concat_axis=0, tiled=True, axis_index_groups=rings)
 
     def a2a(v):
-        return lax.all_to_all(v, "group", split_axis=0, concat_axis=0, tiled=True)
+        return lax.all_to_all(v, "group", split_axis=0, concat_axis=0, tiled=True, axis_index_groups=[peers])
 
     def expert(arrived):
         other = jnp.dot(arrived, w_other, preferred_element_type=f32).astype(bf16)

time: 302 us -> 301 us (level)
  the two profiles are of different devices: /device:TPU:24 before, /device:TPU:145 now
where the time goes in v3:
time: 301 us; the launch traced here: 300 us
  waiting for transfers between devices  205 us (68%)
  starting transfers between devices  41.5 us (14%)
  blocking collectives  30.1 us (10%)
  local copies, waits for them, and re-layouts  10.6 us (4%)
  matrix products  8.67 us (3%)
  other arithmetic  4.16 us (1%)
    all_to_all x2, waiting for transfers between devices, a2a(): lax.all_to_all(v, 'group', split_axis=0, concat_axis=0, tiled=True, axis_...  201 us
    all_to_all x2, starting transfers between devices, a2a(): lax.all_to_all(v, 'group', split_axis=0, concat_axis=0, tiled=True, axis_...  33.5 us
    all_to_all x2, blocking collectives, x_all(): lax.all_to_all(v, 'local', split_axis=0, concat_axis=0, tiled=True, axis_...  30.1 us
    unnamed x28, local copies, waits for them, and re-layouts  7.49 us
  transfers between devices with their start and end apart: 4, of which 4 were waited for; matrix products, arithmetic and copies ran while one was open for 4% of the time, Pallas kernels for 0%

profile of v3, /device:TPU:145, one launch (start us, length us, event | category | flops | bytes accessed | tf_op | source)
XLA Modules:
  0.0 300.1 jit_solution(16557091512363350214)
XLA Ops:
  0.0 0.8 compare_reduce_fusion
  2.1 1.2 pad_maximum_fusion.1
  3.3 26.7 %all-to-all-start = ((bf16[32,16,1024]{2,1,0:T(8,128)(2,1)}), bf16[32,16,1024]{2,1,0:T(8,128)(2,1)S(1)}, u32[]{:S(2)}, u32[]{:S(2)}) async-start(bf16[32,16,1024]{2,1,0:T(8,128)(2,1)} %pad_maximum_fusion.1), calls=%async_computation | async-start | bytes 2097152 | tf_op jit(solution)/shard_map/all_to_all | solution.py:80
  30.1 1.1 bitcast_dynamic-update-slice_fusion.14
  31.4 1.0 bitcast_dynamic-update-slice_fusion.12
  32.4 0.9 bitcast_dynamic-update-slice_fusion.11
  33.3 0.9 bitcast_dynamic-update-slice_fusion.10
  34.2 0.9 bitcast_dynamic-update-slice_fusion.9
  35.1 0.9 bitcast_dynamic-update-slice_fusion.8
  36.0 0.9 bitcast_dynamic-update-slice_fusion.3
  36.8 0.8 bitcast_dynamic-update-slice_fusion.2
  38.4 0.8 bitcast_dynamic-update-slice_fusion
  39.2 95.9 %all-to-all-done = bf16[32,16,1024]{2,1,0:T(8,128)(2,1)S(1)} async-done(((bf16[32,16,1024]{2,1,0:T(8,128)(2,1)}), bf16[32,16,1024]{2,1,0:T(8,128)(2,1)S(1)}, u32[]{:S(2)}, u32[]{:S(2)}) %all-to-all-start) | async-done | bytes 1048608 | tf_op jit(solution)/shard_map/all_to_all | solution.py:80
  135.4 3.1 %convolution_convert_fusion = bf16[576,1024]{1,0:T(8,128)(2,1)S(1)} fusion(bf16[896,1024]{1,0:T(8,128)(2,1)} %bitcast_dynamic-update-slice_fusion, bf16[64,896]{1,0:T(8,128)(2,1)S(1)} %reshape.73, bf16[512,896]{1,0:T(8,128)(2,1)S(1)} %bitcast.93), kind=kOutput, calls=%fused_computation.5 | convolution fusion | flops 1059618816 | bytes 4046848 | tf_op jit(solution)/shard_map/dot_general | solution.py:83
  138.5 3.2 %collective-permute-start = (bf16[576,1024]{1,0:T(8,128)(2,1)S(1)}, bf16[576,1024]{1,0:T(8,128)(2,1)S(1)}, u32[]{:S(2)}, u32[]{:S(2)}) collective-permute-start(bf16[576,1024]{1,0:T(8,128)(2,1)S(1)} %convolution_convert_fusion), channel_id=1, source_target_pairs={{0,4},{4,0},{8,12},{12,8},{16,20},{20,16},{24,28},{28,24},{1,5},{5... | collective-permute-start | bytes 3538952 | tf_op jit(solution)/shard_map/ppermute | solution.py:84
  141.6 2.5 collective-permute-done
  144.1 1.4 add_convert_fusion
  145.8 19.5 %all_to_all.20 = bf16[4,576,256]{2,1,0:T(8,128)(2,1)S(1)} all-to-all(bf16[4,576,256]{2,1,0:T(8,128)(2,1)S(1)} %pad_maximum_fusion), channel_id=1, replica_groups={{0,8,16,24},{4,12,20,28},{1,9,17,25},{5,13,21,29},{2,10,18,26},{6,14,22..., dimensions={0} | all-to-all | bytes 2359296 | tf_op jit(solution)/shard_map/all_to_all | solution.py:77
  165.6 10.7 %all_to_all.21 = bf16[4,576,128]{2,1,0:T(8,128)(2,1)S(1)} all-to-all(bf16[4,576,128]{2,1,0:T(8,128)(2,1)S(1)} %broadcast_in_dim.97), channel_id=1, replica_groups={{0,8,16,24},{4,12,20,28},{1,9,17,25},{5,13,21,29},{2,10,18,26},{6,14,22..., dimensions={0} | all-to-all | bytes 1179648 | tf_op jit(solution)/shard_map/all_to_all | solution.py:77
  176.4 4.9 %collective-permute-start.1 = (bf16[576,512]{1,0:T(8,128)(2,1)S(1)}, bf16[576,512]{1,0:T(8,128)(2,1)S(1)}, u32[]{:S(2)}, u32[]{:S(2)}) collective-permute-start(bf16[576,512]{1,0:T(8,128)(2,1)S(1)} %pad_maximum_fusion.6), channel_id=1, source_target_pairs={{0,4},{4,0},{8,12},{12,8},{16,20},{20,16},{24,28},{28,24},{1,5},{5... | collective-permute-start | bytes 1769480 | tf_op jit(solution)/shard_map/ppermute | solution.py:93
  183.9 1.1 fusion.3
  185.0 6.8 %all-to-all-start.3 = ((bf16[32,16,1024]{2,1,0:T(8,128)(2,1)}), bf16[32,16,1024]{2,1,0:T(8,128)(2,1)S(1)}, u32[]{:S(2)}, u32[]{:S(2)}) async-start(bf16[32,16,1024]{2,1,0:T(8,128)(2,1)} %fusion.3), calls=%async_computation.3 | async-start | bytes 2097152 | tf_op jit(solution)/shard_map/all_to_all | solution.py:80
  192.4 105.6 %all-to-all-done.3 = bf16[32,16,1024]{2,1,0:T(8,128)(2,1)S(1)} async-done(((bf16[32,16,1024]{2,1,0:T(8,128)(2,1)}), bf16[32,16,1024]{2,1,0:T(8,128)(2,1)S(1)}, u32[]{:S(2)}, u32[]{:S(2)}) %all-to-all-start.3) | async-done | bytes 1048608 | tf_op jit(solution)/shard_map/all_to_all | solution.py:80
  299.0 1.1 fusion.1
  (61 shorter events, 7.2 us)
Async XLA Ops:
  0.0 1.2 copy-start
  2.1 27.9 %copy-start.1 = (bf16[1,896,1024]{2,1,0:T(8,128)(2,1)S(1)}, bf16[1,896,1024]{2,1,0:T(8,128)(2,1)}, u32[]{:S(2)}) copy-start(bf16[1,896,1024]{2,1,0:T(8,128)(2,1)} %param.11) | copy-start | bytes 5505028
  3.3 131.9 %all-to-all-start = ((bf16[32,16,1024]{2,1,0:T(8,128)(2,1)}), bf16[32,16,1024]{2,1,0:T(8,128)(2,1)S(1)}, u32[]{:S(2)}, u32[]{:S(2)}) async-start(bf16[32,16,1024]{2,1,0:T(8,128)(2,1)} %pad_maximum_fusion.1), calls=%async_computation | async-start | bytes 2097152 | tf_op jit(solution)/shard_map/all_to_all | solution.py:80
  30.0 3.3 %copy-start.2 = (bf16[1,896,1024]{2,1,0:T(8,128)(2,1)S(1)}, bf16[1,896,1024]{2,1,0:T(8,128)(2,1)}, u32[]{:S(2)}) copy-start(bf16[1,896,1024]{2,1,0:T(8,128)(2,1)} %param.12) | copy-start | bytes 5505028
  36.0 2.4 copy-start.4
  135.4 8.7 %copy-start.5 = (bf16[896,1024]{1,0:T(8,128)(2,1)S(1)}, bf16[896,1024]{1,0:T(8,128)(2,1)}, u32[]{:S(2)}) copy-start(bf16[896,1024]{1,0:T(8,128)(2,1)} %copy-done.4) | copy-start | bytes 5505028
  138.5 5.6 %collective-permute-start = (bf16[576,1024]{1,0:T(8,128)(2,1)S(1)}, bf16[576,1024]{1,0:T(8,128)(2,1)S(1)}, u32[]{:S(2)}, u32[]{:S(2)}) collective-permute-start(bf16[576,1024]{1,0:T(8,128)(2,1)S(1)} %convolution_convert_fusion), channel_id=1, source_target_pairs={{0,4},{4,0},{8,12},{12,8},{16,20},{20,16},{24,28},{28,24},{1,5},{5... | collective-permute-start | bytes 3538952 | tf_op jit(solution)/shard_map/ppermute | solution.py:84
  165.6 15.7 %copy-start.3 = (bf16[1,1024,896]{2,1,0:T(8,128)(2,1)S(1)}, bf16[1,1024,896]{2,1,0:T(8,128)(2,1)}, u32[]{:S(2)}) copy-start(bf16[1,1024,896]{2,1,0:T(8,128)(2,1)} %param.13) | copy-start | bytes 5505028
  176.4 6.5 %collective-permute-start.1 = (bf16[576,512]{1,0:T(8,128)(2,1)S(1)}, bf16[576,512]{1,0:T(8,128)(2,1)S(1)}, u32[]{:S(2)}, u32[]{:S(2)}) collective-permute-start(bf16[576,512]{1,0:T(8,128)(2,1)S(1)} %pad_maximum_fusion.6), channel_id=1, source_target_pairs={{0,4},{4,0},{8,12},{12,8},{16,20},{20,16},{24,28},{28,24},{1,5},{5... | collective-permute-start | bytes 1769480 | tf_op jit(solution)/shard_map/ppermute | solution.py:93
  183.9 8.0 %copy-start.6 = (s32[128,4]{0,1:T(4,128)S(1)}, s32[128,4]{0,1:T(4,128)}, u32[]{:S(2)}) copy-start(s32[128,4]{0,1:T(4,128)} %param.9) | copy-start | bytes 6148
  183.9 8.0 %copy-start.7 = (f32[128,4]{0,1:T(4,128)S(1)}, f32[128,4]{0,1:T(4,128)}, u32[]{:S(2)}) copy-start(f32[128,4]{0,1:T(4,128)} %param.10) | copy-start | bytes 6148
  183.9 8.0 %copy-start.8 = (s32[32]{0:T(128)S(1)}, s32[32]{0:T(128)}, u32[]{:S(2)}) copy-start(s32[32]{0:T(128)} %constant.81.clone) | copy-start | bytes 388
  185.0 112.9 %all-to-all-start.3 = ((bf16[32,16,1024]{2,1,0:T(8,128)(2,1)}), bf16[32,16,1024]{2,1,0:T(8,128)(2,1)S(1)}, u32[]{:S(2)}, u32[]{:S(2)}) async-start(bf16[32,16,1024]{2,1,0:T(8,128)(2,1)} %fusion.3), calls=%async_computation.3 | async-start | bytes 2097152 | tf_op jit(solution)/shard_map/all_to_all | solution.py:80

commit v4 on v3

--- a/solution.py
+++ b/solution.py
@@ -97,14 +97,13 @@
         return out.astype(bf16)
 
     def mix(mixing, rows):
-        out = None
-        left = mixing
+        terms, left = [], mixing
         for _ in range(3):
-            term = lax.reduce_precision(left, 8, 7)
-            left = left - term
-            part = jnp.einsum("ct,cd->td", term.astype(bf16), rows, preferred_element_type=f32)
-            out = part if out is None else out + part
-        return out
+            terms.append(lax.reduce_precision(left, 8, 7))
+            left = left - terms[-1]
+        split = jnp.concatenate(terms, axis=1).astype(bf16)
+        parts = jnp.einsum("cs,cd->sd", split, rows, preferred_element_type=f32)
+        return parts[:tok_rows] + parts[tok_rows : 2 * tok_rows] + parts[2 * tok_rows :]
 
     per = BASE // n_chunks
     extra_match, extra_mixing = rows_of(BASE, n_extra)

time: 301 us -> 300 us (level)
  the two profiles are of different devices: /device:TPU:145 before, /device:TPU:153 now
where the time goes in v4:
time: 300 us
  waiting for transfers between devices  204 us (68%)
  starting transfers between devices  41.5 us (14%)
  blocking collectives  30.1 us (10%)
  local copies, waits for them, and re-layouts  10.5 us (4%)
  matrix products  7.56 us (3%)
  other arithmetic  4.98 us (2%)
    all_to_all x2, waiting for transfers between devices, a2a(): lax.all_to_all(v, 'group', split_axis=0, concat_axis=0, tiled=True, axis_...  201 us
    all_to_all x2, starting transfers between devices, a2a(): lax.all_to_all(v, 'group', split_axis=0, concat_axis=0, tiled=True, axis_...  33.5 us
    all_to_all x2, blocking collectives, x_all(): lax.all_to_all(v, 'local', split_axis=0, concat_axis=0, tiled=True, axis_...  30.1 us
    unnamed x28, local copies, waits for them, and re-layouts  7.49 us
  transfers between devices with their start and end apart: 4, of which 4 were waited for; matrix products, arithmetic and copies ran while one was open for 4% of the time, Pallas kernels for 0%

profile of v4, /device:TPU:153, one launch (start us, length us, event | category | flops | bytes accessed | tf_op | source)
XLA Modules:
  0.0 299.7 jit_solution(11153933023988088945)
XLA Ops:
  0.0 0.8 compare_reduce_fusion
  2.1 1.1 pad_maximum_fusion.1
  3.2 26.7 %all-to-all-start = ((bf16[32,16,1024]{2,1,0:T(8,128)(2,1)}), bf16[32,16,1024]{2,1,0:T(8,128)(2,1)S(1)}, u32[]{:S(2)}, u32[]{:S(2)}) async-start(bf16[32,16,1024]{2,1,0:T(8,128)(2,1)} %pad_maximum_fusion.1), calls=%async_computation | async-start | bytes 2097152 | tf_op jit(solution)/shard_map/all_to_all | solution.py:80
  30.1 1.1 bitcast_dynamic-update-slice_fusion.14
  31.4 1.0 bitcast_dynamic-update-slice_fusion.12
  32.4 0.9 bitcast_dynamic-update-slice_fusion.11
  33.3 0.9 bitcast_dynamic-update-slice_fusion.10
  34.2 0.9 bitcast_dynamic-update-slice_fusion.9
  35.1 0.9 bitcast_dynamic-update-slice_fusion.8
  36.0 0.9 bitcast_dynamic-update-slice_fusion.3
  36.8 0.8 bitcast_dynamic-update-slice_fusion.2
  38.4 0.8 bitcast_dynamic-update-slice_fusion
  39.2 95.9 %all-to-all-done = bf16[32,16,1024]{2,1,0:T(8,128)(2,1)S(1)} async-done(((bf16[32,16,1024]{2,1,0:T(8,128)(2,1)}), bf16[32,16,1024]{2,1,0:T(8,128)(2,1)S(1)}, u32[]{:S(2)}, u32[]{:S(2)}) %all-to-all-start) | async-done | bytes 1048608 | tf_op jit(solution)/shard_map/all_to_all | solution.py:80
  135.4 3.1 %convolution_convert_fusion = bf16[576,1024]{1,0:T(8,128)(2,1)S(1)} fusion(bf16[896,1024]{1,0:T(8,128)(2,1)} %bitcast_dynamic-update-slice_fusion, bf16[64,896]{1,0:T(8,128)(2,1)S(1)} %reshape.73, bf16[512,896]{1,0:T(8,128)(2,1)S(1)} %bitcast.90), kind=kOutput, calls=%fused_computation.5 | convolution fusion | flops 1059618816 | bytes 4046848 | tf_op jit(solution)/shard_map/dot_general | solution.py:83
  138.5 3.2 %collective-permute-start = (bf16[576,1024]{1,0:T(8,128)(2,1)S(1)}, bf16[576,1024]{1,0:T(8,128)(2,1)S(1)}, u32[]{:S(2)}, u32[]{:S(2)}) collective-permute-start(bf16[576,1024]{1,0:T(8,128)(2,1)S(1)} %convolution_convert_fusion), channel_id=1, source_target_pairs={{0,4},{4,0},{8,12},{12,8},{16,20},{20,16},{24,28},{28,24},{1,5},{5... | collective-permute-start | bytes 3538952 | tf_op jit(solution)/shard_map/ppermute | solution.py:84
  141.6 2.5 collective-permute-done
  144.1 1.4 add_convert_fusion
  145.8 19.4 %all_to_all.20 = bf16[4,576,256]{2,1,0:T(8,128)(2,1)S(1)} all-to-all(bf16[4,576,256]{2,1,0:T(8,128)(2,1)S(1)} %pad_maximum_fusion), channel_id=1, replica_groups={{0,8,16,24},{4,12,20,28},{1,9,17,25},{5,13,21,29},{2,10,18,26},{6,14,22..., dimensions={0} | all-to-all | bytes 2359296 | tf_op jit(solution)/shard_map/all_to_all | solution.py:77
  165.6 10.7 %all_to_all.21 = bf16[4,576,128]{2,1,0:T(8,128)(2,1)S(1)} all-to-all(bf16[4,576,128]{2,1,0:T(8,128)(2,1)S(1)} %broadcast_in_dim.97), channel_id=1, replica_groups={{0,8,16,24},{4,12,20,28},{1,9,17,25},{5,13,21,29},{2,10,18,26},{6,14,22..., dimensions={0} | all-to-all | bytes 1179648 | tf_op jit(solution)/shard_map/all_to_all | solution.py:77
  176.4 4.9 %collective-permute-start.1 = (bf16[576,512]{1,0:T(8,128)(2,1)S(1)}, bf16[576,512]{1,0:T(8,128)(2,1)S(1)}, u32[]{:S(2)}, u32[]{:S(2)}) collective-permute-start(bf16[576,512]{1,0:T(8,128)(2,1)S(1)} %pad_maximum_fusion.5), channel_id=1, source_target_pairs={{0,4},{4,0},{8,12},{12,8},{16,20},{20,16},{24,28},{28,24},{1,5},{5... | collective-permute-start | bytes 1769480 | tf_op jit(solution)/shard_map/ppermute | solution.py:93
  182.9 0.8 add_convert_fusion.1
  183.9 1.1 fusion.2
  185.0 6.8 %all-to-all-start.3 = ((bf16[32,16,1024]{2,1,0:T(8,128)(2,1)}), bf16[32,16,1024]{2,1,0:T(8,128)(2,1)S(1)}, u32[]{:S(2)}, u32[]{:S(2)}) async-start(bf16[32,16,1024]{2,1,0:T(8,128)(2,1)} %fusion.2), calls=%async_computation.3 | async-start | bytes 2097152 | tf_op jit(solution)/shard_map/all_to_all | solution.py:80
  192.4 105.5 %all-to-all-done.3 = bf16[32,16,1024]{2,1,0:T(8,128)(2,1)S(1)} async-done(((bf16[32,16,1024]{2,1,0:T(8,128)(2,1)}), bf16[32,16,1024]{2,1,0:T(8,128)(2,1)S(1)}, u32[]{:S(2)}, u32[]{:S(2)}) %all-to-all-start.3) | async-done | bytes 1048608 | tf_op jit(solution)/shard_map/all_to_all | solution.py:80
  (61 shorter events, 7.2 us)
Async XLA Ops:
  0.0 1.2 copy-start
  2.1 27.9 %copy-start.1 = (bf16[1,896,1024]{2,1,0:T(8,128)(2,1)S(1)}, bf16[1,896,1024]{2,1,0:T(8,128)(2,1)}, u32[]{:S(2)}) copy-start(bf16[1,896,1024]{2,1,0:T(8,128)(2,1)} %param.11) | copy-start | bytes 5505028
  3.2 131.9 %all-to-all-start = ((bf16[32,16,1024]{2,1,0:T(8,128)(2,1)}), bf16[32,16,1024]{2,1,0:T(8,128)(2,1)S(1)}, u32[]{:S(2)}, u32[]{:S(2)}) async-start(bf16[32,16,1024]{2,1,0:T(8,128)(2,1)} %pad_maximum_fusion.1), calls=%async_computation | async-start | bytes 2097152 | tf_op jit(solution)/shard_map/all_to_all | solution.py:80
  30.0 3.3 %copy-start.2 = (bf16[1,896,1024]{2,1,0:T(8,128)(2,1)S(1)}, bf16[1,896,1024]{2,1,0:T(8,128)(2,1)}, u32[]{:S(2)}) copy-start(bf16[1,896,1024]{2,1,0:T(8,128)(2,1)} %param.12) | copy-start | bytes 5505028
  36.0 2.4 copy-start.4
  135.4 8.7 %copy-start.5 = (bf16[896,1024]{1,0:T(8,128)(2,1)S(1)}, bf16[896,1024]{1,0:T(8,128)(2,1)}, u32[]{:S(2)}) copy-start(bf16[896,1024]{1,0:T(8,128)(2,1)} %copy-done.4) | copy-start | bytes 5505028
  138.5 5.6 %collective-permute-start = (bf16[576,1024]{1,0:T(8,128)(2,1)S(1)}, bf16[576,1024]{1,0:T(8,128)(2,1)S(1)}, u32[]{:S(2)}, u32[]{:S(2)}) collective-permute-start(bf16[576,1024]{1,0:T(8,128)(2,1)S(1)} %convolution_convert_fusion), channel_id=1, source_target_pairs={{0,4},{4,0},{8,12},{12,8},{16,20},{20,16},{24,28},{28,24},{1,5},{5... | collective-permute-start | bytes 3538952 | tf_op jit(solution)/shard_map/ppermute | solution.py:84
  165.5 15.7 %copy-start.3 = (bf16[1,1024,896]{2,1,0:T(8,128)(2,1)S(1)}, bf16[1,1024,896]{2,1,0:T(8,128)(2,1)}, u32[]{:S(2)}) copy-start(bf16[1,1024,896]{2,1,0:T(8,128)(2,1)} %param.13) | copy-start | bytes 5505028
  176.4 6.5 %collective-permute-start.1 = (bf16[576,512]{1,0:T(8,128)(2,1)S(1)}, bf16[576,512]{1,0:T(8,128)(2,1)S(1)}, u32[]{:S(2)}, u32[]{:S(2)}) collective-permute-start(bf16[576,512]{1,0:T(8,128)(2,1)S(1)} %pad_maximum_fusion.5), channel_id=1, source_target_pairs={{0,4},{4,0},{8,12},{12,8},{16,20},{20,16},{24,28},{28,24},{1,5},{5... | collective-permute-start | bytes 1769480 | tf_op jit(solution)/shard_map/ppermute | solution.py:93
  183.9 8.0 %copy-start.6 = (s32[128,4]{0,1:T(4,128)S(1)}, s32[128,4]{0,1:T(4,128)}, u32[]{:S(2)}) copy-start(s32[128,4]{0,1:T(4,128)} %param.9) | copy-start | bytes 6148
  183.9 8.0 %copy-start.7 = (f32[128,4]{0,1:T(4,128)S(1)}, f32[128,4]{0,1:T(4,128)}, u32[]{:S(2)}) copy-start(f32[128,4]{0,1:T(4,128)} %param.10) | copy-start | bytes 6148
  183.9 8.0 %copy-start.8 = (s32[32]{0:T(128)S(1)}, s32[32]{0:T(128)}, u32[]{:S(2)}) copy-start(s32[32]{0:T(128)} %constant.81.clone) | copy-start | bytes 388
  185.0 112.9 %all-to-all-start.3 = ((bf16[32,16,1024]{2,1,0:T(8,128)(2,1)}), bf16[32,16,1024]{2,1,0:T(8,128)(2,1)S(1)}, u32[]{:S(2)}, u32[]{:S(2)}) async-start(bf16[32,16,1024]{2,1,0:T(8,128)(2,1)} %fusion.2), calls=%async_computation.3 | async-start | bytes 2097152 | tf_op jit(solution)/shard_map/all_to_all | solution.py:80
